TPU v7x, 32 devices: a whole 2x2x4 slice. The times are simulated.
32 devices in a mesh: chain: 8 (over z, y), head: 4 (over x, core).
Axes of the slice: x: 2, y: 2, z: 4, core: 2. Of those that a mesh axis runs over, the one named last changes fastest.
Arguments:
- signal: bfloat16 [4096, 16384], P(('chain', 'head')), may hold values from -6 to 6
- input_map: bfloat16 [4096, 2048], P(('chain', 'head')), may hold values from -0.375 to 0.375
- output_map: bfloat16 [4096, 2048], P(('chain', 'head')), may hold values from -6 to 6
- step_size: bfloat16 [4096, 256], P(('chain', 'head')), may hold values from 0.000625 to 1.61
- decay_rate: float32 [256], replicated, may hold values from 0.1 to 0.3125
- skip_gain: float32 [256], replicated, may hold values from 0.5 to 1.5
Outputs:
- mixed: bfloat16 [4096, 16384], P(('chain', 'head'))
All inputs are finite; a program needn't handle non-finite values.
Results may differ from a plain program's by a relative error of at most 0.0045.
Values may be sent and summed in bfloat16 or wider, within the bound.
A program may use at most 192 MiB of HBM per device.

v0:
```python
import jax
import jax.numpy as jnp
from jax import lax
from jax.sharding import PartitionSpec as P

HEADS = 256
CHANNEL_WIDTH = 64
SSTATE = 256
HEAD_GROUPS = 8
BLOCK = 256


def from_behind(array, axis, by):
    size = lax.axis_size(axis)
    pairs = [(i, i + by) for i in range(size) if 0 <= i + by < size]
    return lax.ppermute(array, axis, pairs)


def prepare(input_c, output_c, step_c, decay_rate, local_heads, group_count):
    chain_rows = input_c.shape[0]
    blocks = chain_rows // BLOCK
    per_group = local_heads // group_count
    head_start = lax.axis_index("head") * local_heads
    head_rates = lax.dynamic_slice_in_dim(decay_rate, head_start, local_heads)
    step_rate = step_c.astype(jnp.float32).reshape(blocks, BLOCK, local_heads)
    cumul = jnp.cumsum(-head_rates * step_rate, axis=1)
    input_groups = input_c.reshape(blocks, BLOCK, group_count, SSTATE)
    output_groups = output_c.reshape(blocks, BLOCK, group_count, SSTATE)
    causal = jnp.arange(BLOCK)[:, None] >= jnp.arange(BLOCK)[None, :]

    def block_weights(pieces):
        cumul_k, step_k, input_k, output_k = pieces
        scores = jnp.einsum("tgn,sgn->gts", output_k, input_k, preferred_element_type=jnp.float32)
        cumul_heads = cumul_k.T.reshape(group_count, per_group, BLOCK)
        differ = jnp.where(causal, cumul_heads[:, :, :, None] - cumul_heads[:, :, None, :], 0.0)
        decays = jnp.where(causal, jnp.exp(differ), 0.0)
        step_heads = step_k.T.reshape(group_count, per_group, 1, BLOCK)
        weights = decays * scores[:, None] * step_heads
        return weights.astype(jnp.bfloat16).reshape(local_heads, BLOCK, BLOCK)

    weights = lax.map(block_weights, (cumul, step_rate, input_groups, output_groups))
    return (step_rate, cumul, input_groups, output_groups, weights)


def finish(signal_c, prepared, skip_gain, local_heads, group_count):
    step_rate, cumul, input_groups, output_groups, weights = prepared
    blocks = cumul.shape[0]
    per_group = local_heads // group_count
    values = signal_c.reshape(blocks, BLOCK, local_heads, CHANNEL_WIDTH)
    values_wide = values.astype(jnp.float32)
    within = jnp.einsum("khts,kshp->kthp", weights, values, preferred_element_type=jnp.float32)
    to_end = jnp.exp(cumul[:, -1:, :] - cumul) * step_rate
    update = (to_end[..., None] * values_wide).astype(jnp.bfloat16)
    update = update.reshape(blocks, BLOCK, group_count, per_group, CHANNEL_WIDTH)
    fresh_state = jnp.einsum(
        "ksgjp,ksgn->kgjpn", update, input_groups, preferred_element_type=jnp.float32
    )
    fresh_state = fresh_state.reshape(blocks, local_heads, CHANNEL_WIDTH, SSTATE)
    block_ends = cumul[:, -1, :]

    def carry_step(carry_state, pieces):
        block_end, fresh_block = pieces
        return (jnp.exp(block_end)[:, None, None] * carry_state + fresh_block, carry_state)

    empty_state = jnp.zeros((local_heads, CHANNEL_WIDTH, SSTATE), jnp.float32)
    final_state, starts = lax.scan(carry_step, empty_state, (block_ends, fresh_state))
    before = jnp.cumsum(block_ends, axis=0) - block_ends
    totals = jnp.sum(block_ends, axis=0)
    chain_len = lax.axis_size("chain")

    def relay_turn(turn_index, arriving):
        leaving = jnp.exp(totals)[:, None, None] * arriving + final_state
        return from_behind(leaving, "chain", 1)

    incoming_state = lax.fori_loop(0, chain_len - 1, relay_turn, jnp.zeros_like(final_state))
    starts = starts + jnp.exp(before)[:, :, None, None] * incoming_state
    rounded = starts.astype(jnp.bfloat16).reshape(
        blocks, group_count, per_group, CHANNEL_WIDTH, SSTATE
    )
    carried = jnp.einsum(
        "ktgn,kgjpn->ktgjp", output_groups, rounded, preferred_element_type=jnp.float32
    )
    carried = carried.reshape(blocks, BLOCK, local_heads, CHANNEL_WIDTH) * jnp.exp(cumul)[..., None]
    head_start = lax.axis_index("head") * local_heads
    gain_heads = lax.dynamic_slice_in_dim(skip_gain, head_start, local_heads)
    result = (within + carried + gain_heads[:, None] * values_wide).astype(jnp.bfloat16)
    result = result.reshape(blocks * BLOCK, local_heads * CHANNEL_WIDTH)
    return lax.all_to_all(result, "head", split_axis=0, concat_axis=1, tiled=True)


def shards(signal, input_map, output_map, step_size, decay_rate, skip_gain):
    head_count = lax.axis_size("head")
    local_heads = HEADS // head_count
    group_heads = HEADS // HEAD_GROUPS
    group_count = max(1, local_heads // group_heads)
    copies = max(1, group_heads // local_heads)
    row_count = signal.shape[0]
    input_rep = jnp.repeat(
        input_map.reshape(row_count, HEAD_GROUPS, SSTATE), copies, axis=1
    ).reshape(row_count, -1)
    output_rep = jnp.repeat(
        output_map.reshape(row_count, HEAD_GROUPS, SSTATE), copies, axis=1
    ).reshape(row_count, -1)
    signal_c, input_c, output_c, step_c = (
        lax.all_to_all(signal, "head", split_axis=1, concat_axis=0, tiled=True),
        lax.all_to_all(input_rep, "head", split_axis=1, concat_axis=0, tiled=True),
        lax.all_to_all(output_rep, "head", split_axis=1, concat_axis=0, tiled=True),
        lax.all_to_all(step_size, "head", split_axis=1, concat_axis=0, tiled=True),
    )
    prepared = prepare(input_c, output_c, step_c, decay_rate, local_heads, group_count)
    return finish(signal_c, prepared, skip_gain, local_heads, group_count)


def solution(mesh):
    return jax.shard_map(
        shards,
        mesh=mesh,
        in_specs=(
            P(("chain", "head"), None),
            P(("chain", "head"), None),
            P(("chain", "head"), None),
            P(("chain", "head"), None),
            P(),
            P(),
        ),
        out_specs=P(("chain", "head"), None),
        check_vma=False,
    )
```

profile of v0, /device:TPU:1, one launch (start us, length us, event | category | flops | bytes accessed | tf_op | source)
XLA Modules:
  0.0 962.7 jit_solution(13392410668254311873)
XLA Ops:
  0.0 1.6 copy.77
  1.6 4.3 all-to-all-start
  5.8 0.8 dynamic-slice_negate_fusion
  6.6 6.5 copy.86
  13.1 0.9 copy.134
  13.9 0.9 copy.135
  14.9 3.5 all-to-all-start.2
  18.9 1.2 reduce-window.6
  20.9 5.3 all-to-all-done.2
  26.3 4.3 all-to-all-start.1
  30.7 7.8 all-to-all-done.1
  38.6 5.7 all-to-all-start.3
  44.4 19.1 %while.38 = (s32[]{:T(128)}, bf16[2,64,256,256]{3,2,1,0:T(8,128)(2,1)}, f32[2,256,64]{1,2,0:T(8,128)S(1)}, bf16[2,256,2,256]{3,2,1,0:T(2,128)(2,1)S(1)}, bf16[2,...) while((s32[]{:T(128)}, ...), condition=%wide.region_3.4_spmd.clone.clone, body=%wide.region_2.3_spmd.clone.clone.sunk | while | flops 92340224 | bytes 45154900 | solution.py:41
  45.0 2.0 mul.179
  47.1 6.8 fusion.27
  54.5 2.0 mul.179
  56.6 6.9 fusion.27
  63.5 28.2 %all-to-all-done.3 = bf16[128,4,4096]{0,2,1:T(8,128)(2,1)} async-done(((bf16[128,4,4096]{0,2,1:T(8,128)(2,1)}), bf16[128,4,4096]{0,2,1:T(8,128)(2,1)}, u32[]{:S(2)}, u32[]{:S(2)}) %all-to-all-start.3) | async-done | bytes 4194336 | tf_op jit(solution)/shard_map/all_to_all | solution.py:105
  91.6 2.7 bitcast_convert_fusion
  94.4 18.6 %copy.91 = f32[4,128,4096]{1,0,2:T(4,128)} copy(f32[4,128,4096]{1,2,0:T(8,128)S(1)} %bitcast_convert_fusion) | data formatting | bytes 16777216 | tf_op jit(solution)/shard_map/convert_element_type | solution.py:50
  113.0 11.9 %reshape.155 = f32[2,256,2,32,64]{1,0,4,3,2:T(2,128)} reshape(f32[4,128,4096]{1,0,2:T(4,128)} %copy.91) | data formatting | bytes 16777216 | tf_op jit(solution)/shard_map/convert_element_type | solution.py:50
  124.9 10.1 %multiply_convert_fusion = bf16[2,256,2,32,64]{1,0,4,3,2:T(2,128)(2,1)} fusion(f32[2,256,2,32,64]{1,0,4,3,2:T(2,128)} %reshape.155, f32[2,256,2,32]{1,0,3,2:T(2,128)S(1)} %copy.90), kind=kLoop, calls=%fused_computation.23 | loop fusion | flops 4194304 | bytes 12713984 | tf_op jit(solution)/shard_map/convert_element_type | solution.py:53
  135.0 6.7 fusion.10
  141.7 18.4 %while.39 = (s32[]{:T(128)}, f32[64,64,256]{2,1,0:T(8,128)}, f32[2,64,64,256]{3,2,1,0:T(8,128)}, f32[2,64]{1,0:T(2,128)S(1)}, f32[2,64,64,256]{3,2,1,0:T(8,128)}, /*index=5*/s32[]{:T(128)}, s32[]{:T(128)}) while((s32[]{:T(128)}, f32[64,64,256]{2,1,0:T(8,128)}, f32[2,64,64,256]{3,2,1,0:T(8,128)}, f32[2,64]{1,0:T(2,128)S(1)}, ...), condition=%wide.region_5.6_spmd.clone, body=%wide.region_4.5_spmd.clone.sunk | while | flops 4194307 | bytes 54527352 | solution.py:66
  141.7 2.7 bitcast_dynamic-update-slice_fusion.2
  144.4 2.2 copy-done
  146.6 2.6 bitcast_add_fusion.3
  149.2 5.0 bitcast_dynamic-update-slice_fusion.2
  154.2 1.1 copy-done
  155.4 4.8 bitcast_add_fusion.3
  160.1 7.6 copy.87
  167.7 9.8 %reshape.150 = bf16[2,256,64,64]{1,0,3,2:T(2,128)(2,1)} reshape(bf16[4,128,4096]{1,0,2:T(4,128)(2,1)} %copy.87) | data formatting | bytes 8388608 | tf_op jit(solution)/shard_map/reshape | solution.py:49
  177.5 2.6 broadcast.68
  180.0 678.7 %while.37 = (s32[]{:T(128)}, f32[64,64,256]{2,1,0:T(8,128)}, f32[64,1,1]{0,2,1:T(1,128)S(1)}, f32[64,64,256]{2,1,0:T(8,128)}, s32[]{:T(128)}) while((s32[]{:T(128)}, f32[64,64,256]{2,1,0:T(8,128)}, f32[64,1,1]{0,2,1:T(1,128)S(1)}, f32[64,64,256]{2,1,0:T(8,128)}, s32[]{:T(128)}) %tuple.77), condition=%wide.region_9.10_spmd, body=%wide.region_8.9_spmd.sunk | while | flops 2097154 | bytes 29360484 | solution.py:75
  180.0 5.9 multiply_add_fusion.2
  185.9 5.7 collective-permute-start
  191.6 87.2 %collective-permute-done = f32[64,64,256]{2,1,0:T(8,128)} collective-permute-done((f32[64,64,256]{2,1,0:T(8,128)}, f32[64,64,256]{2,1,0:T(8,128)}, u32[]{:S(2)}, u32[]{:S(2)}) %collective-permute-start) | collective-permute-done | bytes 4194336 | tf_op jit(solution)/shard_map/while/body/eval_jaxpr/ppermute | solution.py:16
  278.9 5.9 multiply_add_fusion.2
  284.7 6.2 collective-permute-start
  290.9 86.3 %collective-permute-done = f32[64,64,256]{2,1,0:T(8,128)} collective-permute-done((f32[64,64,256]{2,1,0:T(8,128)}, f32[64,64,256]{2,1,0:T(8,128)}, u32[]{:S(2)}, u32[]{:S(2)}) %collective-permute-start) | collective-permute-done | bytes 4194336 | tf_op jit(solution)/shard_map/while/body/eval_jaxpr/ppermute | solution.py:16
  377.2 5.9 multiply_add_fusion.2
  383.1 6.2 collective-permute-start
  389.2 85.4 %collective-permute-done = f32[64,64,256]{2,1,0:T(8,128)} collective-permute-done((f32[64,64,256]{2,1,0:T(8,128)}, f32[64,64,256]{2,1,0:T(8,128)}, u32[]{:S(2)}, u32[]{:S(2)}) %collective-permute-start) | collective-permute-done | bytes 4194336 | tf_op jit(solution)/shard_map/while/body/eval_jaxpr/ppermute | solution.py:16
  474.7 5.9 multiply_add_fusion.2
  480.5 7.0 collective-permute-start
  487.5 84.5 %collective-permute-done = f32[64,64,256]{2,1,0:T(8,128)} collective-permute-done((f32[64,64,256]{2,1,0:T(8,128)}, f32[64,64,256]{2,1,0:T(8,128)}, u32[]{:S(2)}, u32[]{:S(2)}) %collective-permute-start) | collective-permute-done | bytes 4194336 | tf_op jit(solution)/shard_map/while/body/eval_jaxpr/ppermute | solution.py:16
  572.0 5.9 multiply_add_fusion.2
  577.9 7.1 collective-permute-start
  584.9 83.6 %collective-permute-done = f32[64,64,256]{2,1,0:T(8,128)} collective-permute-done((f32[64,64,256]{2,1,0:T(8,128)}, f32[64,64,256]{2,1,0:T(8,128)}, u32[]{:S(2)}, u32[]{:S(2)}) %collective-permute-start) | collective-permute-done | bytes 4194336 | tf_op jit(solution)/shard_map/while/body/eval_jaxpr/ppermute | solution.py:16
  668.5 5.9 multiply_add_fusion.2
  674.4 7.1 collective-permute-start
  681.4 82.6 %collective-permute-done = f32[64,64,256]{2,1,0:T(8,128)} collective-permute-done((f32[64,64,256]{2,1,0:T(8,128)}, f32[64,64,256]{2,1,0:T(8,128)}, u32[]{:S(2)}, u32[]{:S(2)}) %collective-permute-start) | collective-permute-done | bytes 4194336 | tf_op jit(solution)/shard_map/while/body/eval_jaxpr/ppermute | solution.py:16
  764.1 5.9 multiply_add_fusion.2
  770.0 7.1 collective-permute-start
  777.0 81.7 %collective-permute-done = f32[64,64,256]{2,1,0:T(8,128)} collective-permute-done((f32[64,64,256]{2,1,0:T(8,128)}, f32[64,64,256]{2,1,0:T(8,128)}, u32[]{:S(2)}, u32[]{:S(2)}) %collective-permute-start) | collective-permute-done | bytes 4194336 | tf_op jit(solution)/shard_map/while/body/eval_jaxpr/ppermute | solution.py:16
  858.7 5.2 add_convert_fusion
  863.9 1.3 fusion.16
  865.2 0.9 copy-done.1
  866.1 10.0 %fusion.9 = bf16[2,256,64,64]{1,3,2,0:T(8,128)(2,1)} fusion(f32[2,256,64,64]{1,3,2,0:T(8,128)S(1)} %bitcast.113, f32[64]{0:T(128)S(1)} %dynamic_slice.29, f32[2,256,64]{1,2,0:T(8,128)S(1)} %get-tuple-element.239, bf16[2,256,64,64]{1,0,3,2:T(2,128)(2,1)S(1)} %copy-done.1, bf16[2,64,256,256]{3,2,1,0:T(8,128)(2,1)} %get-tuple-element.123), kind=kOutput, calls=%fused_computation.21 | convolution fusion | flops 1086324736 | bytes 33685760 | tf_op jit(solution)/shard_map/khts,kshp->kthp/dot_general | solution.py:51
  876.1 8.5 copy.96
  884.6 10.9 %all_to_all.71 = bf16[4,128,4096]{1,0,2:T(4,128)(2,1)} reshape(bf16[2,256,64,64]{1,0,3,2:T(2,128)(2,1)} %copy.96) | data formatting | bytes 8388608 | tf_op jit(solution)/shard_map/all_to_all | solution.py:88
  895.5 2.7 copy.97
  898.2 58.1 %all_to_all.80 = bf16[4,128,4096]{1,2,0:T(8,128)(2,1)} all-to-all(bf16[4,128,4096]{1,2,0:T(8,128)(2,1)S(1)} %copy.97), channel_id=1, replica_groups=mesh['chain'=8,'head'=4] {'head'}, dimensions={0} | all-to-all | bytes 8388608 | tf_op jit(solution)/shard_map/all_to_all | solution.py:88
  956.3 6.4 copy.98
  (46 shorter events, 3.0 us)
Async XLA Ops:
  1.6 13.3 %all-to-all-start = ((bf16[128,4,64]{0,2,1:T(8,128)(2,1)}), bf16[128,4,64]{0,2,1:T(8,128)(2,1)S(1)}, u32[]{:S(2)}, u32[]{:S(2)}) async-start(bf16[128,4,64]{0,2,1:T(8,128)(2,1)} %bitcast.1), calls=%async_computation | async-start | bytes 131072 | tf_op jit(solution)/shard_map/all_to_all | solution.py:108
  6.6 6.5 copy-start.4
  6.6 7.3 copy-start.5
  6.6 8.2 copy-start.6
  14.9 11.4 %all-to-all-start.2 = ((bf16[128,4,512]{2,0,1:T(8,128)(2,1)}), bf16[128,4,512]{2,0,1:T(8,128)(2,1)S(1)}, u32[]{:S(2)}, u32[]{:S(2)}) async-start(bf16[128,4,512]{2,0,1:T(8,128)(2,1)} %bitcast.93), calls=%async_computation.2 | async-start | bytes 1048576 | tf_op jit(solution)/shard_map/all_to_all | solution.py:106
  26.3 12.3 %all-to-all-start.1 = ((bf16[128,4,512]{2,0,1:T(8,128)(2,1)}), bf16[128,4,512]{2,0,1:T(8,128)(2,1)S(1)}, u32[]{:S(2)}, u32[]{:S(2)}) async-start(bf16[128,4,512]{2,0,1:T(8,128)(2,1)} %bitcast.94), calls=%async_computation.1 | async-start | bytes 1048576 | tf_op jit(solution)/shard_map/all_to_all | solution.py:107
  38.6 53.1 %all-to-all-start.3 = ((bf16[128,4,4096]{0,2,1:T(8,128)(2,1)}), bf16[128,4,4096]{0,2,1:T(8,128)(2,1)}, u32[]{:S(2)}, u32[]{:S(2)}) async-start(bf16[128,4,4096]{0,2,1:T(8,128)(2,1)} %bitcast.114), calls=%async_computation.3 | async-start | bytes 8388608 | tf_op jit(solution)/shard_map/all_to_all | solution.py:105
  63.5 30.9 %copy-start.2 = (bf16[2,256,2,256]{3,2,1,0:T(2,128)(2,1)}, bf16[2,256,2,256]{3,2,1,0:T(2,128)(2,1)S(1)}, u32[]{:S(2)}) copy-start(bf16[2,256,2,256]{3,2,1,0:T(2,128)(2,1)S(1)} %get-tuple-element.400) | copy-start | bytes 1572868
  141.7 4.9 copy-start
  149.2 6.2 copy-start
  185.9 93.0 %collective-permute-start = (f32[64,64,256]{2,1,0:T(8,128)}, f32[64,64,256]{2,1,0:T(8,128)}, u32[]{:S(2)}, u32[]{:S(2)}) collective-permute-start(f32[64,64,256]{2,1,0:T(8,128)} %multiply_add_fusion.2), channel_id=1, source_target_pairs={{0,4},{4,8},{8,12},{12,16},{16,20},{20,24},{24,28},{1,5},{5,9},{9,... | collective-permute-start | bytes 12582920 | tf_op jit(solution)/shard_map/while/body/eval_jaxpr/ppermute | solution.py:16
  284.7 92.5 %collective-permute-start = (f32[64,64,256]{2,1,0:T(8,128)}, f32[64,64,256]{2,1,0:T(8,128)}, u32[]{:S(2)}, u32[]{:S(2)}) collective-permute-start(f32[64,64,256]{2,1,0:T(8,128)} %multiply_add_fusion.2), channel_id=1, source_target_pairs={{0,4},{4,8},{8,12},{12,16},{16,20},{20,24},{24,28},{1,5},{5,9},{9,... | collective-permute-start | bytes 12582920 | tf_op jit(solution)/shard_map/while/body/eval_jaxpr/ppermute | solution.py:16
  383.1 91.6 %collective-permute-start = (f32[64,64,256]{2,1,0:T(8,128)}, f32[64,64,256]{2,1,0:T(8,128)}, u32[]{:S(2)}, u32[]{:S(2)}) collective-permute-start(f32[64,64,256]{2,1,0:T(8,128)} %multiply_add_fusion.2), channel_id=1, source_target_pairs={{0,4},{4,8},{8,12},{12,16},{16,20},{20,24},{24,28},{1,5},{5,9},{9,... | collective-permute-start | bytes 12582920 | tf_op jit(solution)/shard_map/while/body/eval_jaxpr/ppermute | solution.py:16
  480.5 91.5 %collective-permute-start = (f32[64,64,256]{2,1,0:T(8,128)}, f32[64,64,256]{2,1,0:T(8,128)}, u32[]{:S(2)}, u32[]{:S(2)}) collective-permute-start(f32[64,64,256]{2,1,0:T(8,128)} %multiply_add_fusion.2), channel_id=1, source_target_pairs={{0,4},{4,8},{8,12},{12,16},{16,20},{20,24},{24,28},{1,5},{5,9},{9,... | collective-permute-start | bytes 12582920 | tf_op jit(solution)/shard_map/while/body/eval_jaxpr/ppermute | solution.py:16
  577.9 90.6 %collective-permute-start = (f32[64,64,256]{2,1,0:T(8,128)}, f32[64,64,256]{2,1,0:T(8,128)}, u32[]{:S(2)}, u32[]{:S(2)}) collective-permute-start(f32[64,64,256]{2,1,0:T(8,128)} %multiply_add_fusion.2), channel_id=1, source_target_pairs={{0,4},{4,8},{8,12},{12,16},{16,20},{20,24},{24,28},{1,5},{5,9},{9,... | collective-permute-start | bytes 12582920 | tf_op jit(solution)/shard_map/while/body/eval_jaxpr/ppermute | solution.py:16
  674.4 89.7 %collective-permute-start = (f32[64,64,256]{2,1,0:T(8,128)}, f32[64,64,256]{2,1,0:T(8,128)}, u32[]{:S(2)}, u32[]{:S(2)}) collective-permute-start(f32[64,64,256]{2,1,0:T(8,128)} %multiply_add_fusion.2), channel_id=1, source_target_pairs={{0,4},{4,8},{8,12},{12,16},{16,20},{20,24},{24,28},{1,5},{5,9},{9,... | collective-permute-start | bytes 12582920 | tf_op jit(solution)/shard_map/while/body/eval_jaxpr/ppermute | solution.py:16
  770.0 88.8 %collective-permute-start = (f32[64,64,256]{2,1,0:T(8,128)}, f32[64,64,256]{2,1,0:T(8,128)}, u32[]{:S(2)}, u32[]{:S(2)}) collective-permute-start(f32[64,64,256]{2,1,0:T(8,128)} %multiply_add_fusion.2), channel_id=1, source_target_pairs={{0,4},{4,8},{8,12},{12,16},{16,20},{20,24},{24,28},{1,5},{5,9},{9,... | collective-permute-start | bytes 12582920 | tf_op jit(solution)/shard_map/while/body/eval_jaxpr/ppermute | solution.py:16
  858.7 5.2 copy-start.3
  863.9 2.2 copy-start.1
where the time goes:
time: 968 us; the launch traced here: 963 us
  waiting for transfers between devices  633 us (65%)
  local copies, waits for them, and re-layouts  98.7 us (10%)
  other arithmetic  90.5 us (9%)
  starting transfers between devices  63.9 us (7%)
  blocking collectives  58.1 us (6%)
  matrix products  18.4 us (2%)
    ppermute x7, waiting for transfers between devices, from_behind(): return lax.ppermute(array, axis, pairs)  591 us
    all_to_all x1, blocking collectives, finish(): lax.all_to_all(result, 'head', split_axis=0, concat_axis=1, tiled=True)  58.1 us
    ppermute x7, starting transfers between devices, from_behind(): return lax.ppermute(array, axis, pairs)  46.2 us
    add x7, other arithmetic, relay_turn(): leaving = jnp.exp(totals)[:, None, None] * arriving + final_state  41.1 us
    convert_element_type x2, local copies, waits for them, and re-layouts, finish(): values_wide = values.astype(jnp.float32)  30.5 us
    all_to_all x1, waiting for transfers between devices, shards(): lax.all_to_all(signal, 'head', split_axis=1, concat_axis=0, tiled=True)  28.2 us
    all_to_all x3, local copies, waits for them, and re-layouts, finish(): lax.all_to_all(result, 'head', split_axis=0, concat_axis=1, tiled=True)  19.9 us
  transfers between devices with their start and end apart: 11, of which 10 were waited for; matrix products, arithmetic and copies ran while one was open for 3% of the time, Pallas kernels for 0%

commit v1 on v0

v1 whole, which is shorter than its diff:
```python
import functools
import math

import jax
import jax.numpy as jnp
from jax import lax
from jax.experimental import pallas as pl
from jax.experimental.pallas import tpu as pltpu
from jax.sharding import PartitionSpec as P

HEADS = 256
CHANNEL_WIDTH = 64
SSTATE = 256
HEAD_GROUPS = 8
BLOCK = 256
GROUP_HEADS = HEADS // HEAD_GROUPS
PART_HEADS = 4
PART = PART_HEADS * CHANNEL_WIDTH
LOG2E = 1.0 / math.log(2.0)
MESH = pl.DeviceIdType.MESH


def dot(a, b):
    return jnp.dot(a, b, preferred_element_type=jnp.float32)


def kernel(
    head_len, chain_len,
    signal, in_map, out_map, step, rate_row, skip_row, mixed,
    sig_buf, in_buf, out_map_buf, step_buf, u_rows, scores, in_t, cols_ref,
    states, befores, partial_out, grow, out_buf, arriving, leaving,
    meta_local, meta_send, meta_recv, sig_local, sig_send, sig_recv,
    state_send, state_recv, out_local, out_send, out_recv,
):
    me = lax.axis_index("head")
    pos = lax.axis_index("chain")
    rows = signal.shape[0]
    local_heads = HEADS // head_len
    cols = local_heads * CHANNEL_WIDTH
    parts = cols // PART
    groups = max(1, local_heads // GROUP_HEADS)
    map_cols = groups * SSTATE
    blocks = rows * head_len // BLOCK

    def head_peer(r):
        return lax.rem(me + r, head_len)

    barrier = pltpu.get_barrier_semaphore()
    for r in range(1, head_len):
        pl.semaphore_signal(barrier, inc=1, device_id={"head": head_peer(r)}, device_id_type=MESH)
    for d in (1, chain_len - 1):
        pl.semaphore_signal(
            barrier, inc=1, device_id={"chain": lax.rem(pos + d, chain_len)}, device_id_type=MESH
        )

    my_rows = pl.ds(pl.multiple_of(me * rows, rows), rows)

    def map_cols_of(peer):
        start = (peer * local_heads) // GROUP_HEADS * SSTATE
        return pl.ds(pl.multiple_of(start, SSTATE), map_cols)

    def part_cols(j):
        return pl.ds(pl.multiple_of(j * PART, PART), PART)

    def wide_cols(peer, j):
        return pl.ds(pl.multiple_of(peer * cols + j * PART, PART), PART)

    def meta_pairs(peer):
        return (
            (step, step_buf.at[my_rows, :]),
            (in_map.at[:, map_cols_of(peer)], in_buf.at[my_rows, :]),
            (out_map.at[:, map_cols_of(peer)], out_map_buf.at[my_rows, :]),
        )

    def meta_copy(r, i):
        src, dst = meta_pairs(head_peer(r))[i]
        return pltpu.make_async_remote_copy(
            src_ref=src, dst_ref=dst, send_sem=meta_send.at[i, r], recv_sem=meta_recv.at[i, r],
            device_id={"head": head_peer(r)}, device_id_type=MESH,
        )

    def meta_own(i):
        src, dst = meta_pairs(me)[i]
        return pltpu.make_async_copy(src, dst, meta_local.at[i])

    def sig_own():
        src = signal.at[:, pl.ds(pl.multiple_of(me * cols, PART), cols)]
        return pltpu.make_async_copy(src, sig_buf.at[my_rows, :], sig_local)

    def sig_copy(j, r):
        return pltpu.make_async_remote_copy(
            src_ref=signal.at[:, wide_cols(head_peer(r), j)],
            dst_ref=sig_buf.at[my_rows, part_cols(j)],
            send_sem=sig_send.at[j, r], recv_sem=sig_recv.at[j, r],
            device_id={"head": head_peer(r)}, device_id_type=MESH,
        )

    def state_copy(j):
        return pltpu.make_async_remote_copy(
            src_ref=leaving.at[:, part_cols(j)], dst_ref=arriving.at[:, part_cols(j)],
            send_sem=state_send.at[j], recv_sem=state_recv.at[j],
            device_id={"chain": lax.rem(pos + 1, chain_len)}, device_id_type=MESH,
        )

    def out_copy(j, r):
        peer = head_peer(r)
        return pltpu.make_async_remote_copy(
            src_ref=out_buf.at[pl.ds(pl.multiple_of(peer * rows, rows), rows), part_cols(j)],
            dst_ref=mixed.at[:, wide_cols(me, j)],
            send_sem=out_send.at[j, r], recv_sem=out_recv.at[j, r],
            device_id={"head": peer}, device_id_type=MESH,
        )

    def out_own(j):
        return pltpu.make_async_copy(
            out_buf.at[my_rows, part_cols(j)], mixed.at[:, wide_cols(me, j)], out_local.at[j]
        )

    for i in range(3):
        meta_own(i).start()
    sig_own().start()
    pl.semaphore_wait(barrier, head_len + 1)
    for i in range(3):
        for r in range(1, head_len):
            meta_copy(r, i).start()

    def send_signal(j, _):
        for r in range(1, head_len):
            sig_copy(j, r).start()
        return 0

    lax.fori_loop(0, parts, send_signal, 0)

    first = lax.broadcasted_iota(jnp.int32, (BLOCK, BLOCK), 0)
    second = lax.broadcasted_iota(jnp.int32, (BLOCK, BLOCK), 1)
    eye = first == second
    cols_ref[:, 0:1] = jnp.sum(jnp.where(eye, rate_row[...], 0.0), axis=1, keepdims=True)
    cols_ref[:, 1:2] = jnp.sum(jnp.where(eye, skip_row[...], 0.0), axis=1, keepdims=True)

    for i in range(3):
        meta_own(i).wait()
        for r in range(1, head_len):
            meta_copy(r, i).wait_recv()
    sig_own().wait()

    def block_rows(b):
        return pl.ds(pl.multiple_of(b * BLOCK, BLOCK), BLOCK)

    def prepare(b, _):
        until = (first <= second).astype(jnp.float32).astype(jnp.bfloat16)
        step_t = jnp.transpose(step_buf[block_rows(b), :].astype(jnp.float32))
        sums = dot(step_t.astype(jnp.bfloat16), until)
        u_rows[b] = (-cols_ref[:, 0:1] * sums - jnp.log(step_t)) * LOG2E
        for g in range(groups):
            window = slice(g * SSTATE, (g + 1) * SSTATE)
            in_g = in_buf[block_rows(b), window]
            in_gt = jnp.transpose(in_g.astype(jnp.float32)).astype(jnp.bfloat16)
            in_t[b * groups + g] = in_gt
            scores[b * groups + g] = jnp.where(
                first >= second, dot(out_map_buf[block_rows(b), window], in_gt), 0.0
            )
        return 0

    lax.fori_loop(0, blocks, prepare, 0)

    half = BLOCK // 2
    low_lane = lax.broadcasted_iota(jnp.int32, (BLOCK, 128), 1) < CHANNEL_WIDTH
    low_row = lax.broadcasted_iota(jnp.int32, (1, 128), 1) < CHANNEL_WIDTH

    def local_part(j):
        for r in range(1, head_len):
            sig_copy(j, r).wait_recv()
        group = (j * PART_HEADS) // GROUP_HEADS
        head0 = me * local_heads + j * PART_HEADS
        spread = lax.broadcasted_iota(jnp.int32, (HEADS, PART_HEADS * 128), 1) // 128
        chosen = lax.broadcasted_iota(jnp.int32, (HEADS, PART_HEADS * 128), 0) == head0 + spread
        pick = chosen.astype(jnp.float32).astype(jnp.bfloat16)
        slope = jnp.sum(jnp.where(chosen, cols_ref[:, 0:1], 0.0), axis=0, keepdims=True) * -LOG2E
        gains = jnp.sum(jnp.where(chosen, cols_ref[:, 1:2], 0.0), axis=0, keepdims=True)
        lower = (first >= second).astype(jnp.float32).astype(jnp.bfloat16)
        states[0, :, part_cols(j)] = jnp.zeros((SSTATE, PART), jnp.float32)
        befores[0, :, part_cols(j)] = jnp.zeros((8, PART), jnp.float32)

        def one_block(b, _):
            here = block_rows(b)
            wide_step = dot(step_buf[here, :], pick)
            cumul = dot(lower, wide_step.astype(jnp.bfloat16)) * slope
            log_step = jnp.log(wide_step) * LOG2E
            score = b * groups + group
            for q in range(PART_HEADS // 2):
                at = pl.ds(pl.multiple_of(j * PART + q * 128, 128), 128)
                values = sig_buf[here, at]
                wide_values = values.astype(jnp.float32)
                gain = jnp.where(
                    low_row, gains[:, 256 * q:256 * q + 128], gains[:, 256 * q + 128:256 * q + 256]
                )
                total = gain * wide_values
                top, bottom = total[:half], total[half:]
                for k in range(2):
                    h = 2 * q + k
                    mask = low_lane if k == 0 else jnp.logical_not(low_lane)
                    own = jnp.where(mask, wide_values, 0.0).astype(jnp.bfloat16)
                    cumul_h = cumul[:, 128 * h:128 * h + 128]
                    row = u_rows[b, pl.ds(head0 + h, 1), :]
                    near = jnp.exp2(jnp.minimum(cumul_h - row[:, :half], 1.0))
                    near = (near * scores[score, :, :half]).astype(jnp.bfloat16)
                    far = jnp.exp2(jnp.minimum(cumul_h[half:] - row[:, half:], 1.0))
                    far = (far * scores[score, half:, half:]).astype(jnp.bfloat16)
                    near_sum = dot(near, own[:half])
                    top = top + near_sum[:half]
                    bottom = bottom + near_sum[half:] + dot(far, own[half:])
                base = pl.multiple_of(b * BLOCK, BLOCK)
                partial_out[pl.ds(base, half), at] = top
                partial_out[pl.ds(base + half, half), at] = bottom
                pair = slice(256 * q, 256 * q + 128), slice(256 * q + 128, 256 * q + 256)
                cumul_p = jnp.where(low_lane, cumul[:, pair[0]], cumul[:, pair[1]])
                log_p = jnp.where(low_lane, log_step[:, pair[0]], log_step[:, pair[1]])
                end = cumul_p[BLOCK - 1:BLOCK, :]
                grow[here, at] = jnp.exp2(cumul_p)
                update = (jnp.exp2(end - cumul_p + log_p) * wide_values).astype(jnp.bfloat16)
                fresh = dot(in_t[score], update)
                states[b + 1, :, at] = jnp.exp2(end) * states[b, :, at] + fresh
                befores[b + 1, :, at] = befores[b, :, at] + end
            return 0

        lax.fori_loop(0, blocks, one_block, 0)

    def carried_part(j):
        at = part_cols(j)
        group = (j * PART_HEADS) // GROUP_HEADS

        @pl.when(pos > 0)
        def _():
            state_copy(j).wait_recv()

        @pl.when(pos == 0)
        def _():
            arriving[:, at] = jnp.zeros((SSTATE, PART), jnp.bfloat16)

        @pl.when(pos < chain_len - 1)
        def _():
            before = arriving[:, at].astype(jnp.float32)
            after = jnp.exp2(befores[blocks, 0:1, at]) * before + states[blocks, :, at]
            leaving[:, at] = after.astype(jnp.bfloat16)
            state_copy(j).start()

        def one_block(b, _):
            here = block_rows(b)
            before = arriving[:, at].astype(jnp.float32)
            state = jnp.exp2(befores[b, 0:1, at]) * before + states[b, :, at]
            maps = out_map_buf[here, pl.ds(pl.multiple_of(group * SSTATE, SSTATE), SSTATE)]
            carried = dot(maps, state.astype(jnp.bfloat16)) * grow[here, at]
            out_buf[here, at] = (partial_out[here, at] + carried).astype(jnp.bfloat16)
            return 0

        lax.fori_loop(0, blocks, one_block, 0)
        for r in range(1, head_len):
            out_copy(j, r).start()
        out_own(j).start()

    def turn(i, _):
        @pl.when(i < parts)
        def _():
            local_part(i)

        @pl.when(jnp.logical_and(i >= pos, i < pos + parts))
        def _():
            carried_part(i - pos)

        return 0

    lax.fori_loop(0, parts + chain_len - 1, turn, 0)

    for i in range(3):
        for r in range(1, head_len):
            meta_copy(r, i).wait_send()

    def settle(j, _):
        for r in range(1, head_len):
            sig_copy(j, r).wait_send()
            out_copy(j, r).wait()
        out_own(j).wait()

        @pl.when(pos < chain_len - 1)
        def _():
            state_copy(j).wait_send()

        return 0

    lax.fori_loop(0, parts, settle, 0)


def shards(signal, input_map, output_map, step_size, decay_rate, skip_gain):
    head_len = lax.axis_size("head")
    chain_len = lax.axis_size("chain")
    rows = signal.shape[0]
    local_heads = HEADS // head_len
    cols = local_heads * CHANNEL_WIDTH
    parts = cols // PART
    groups = max(1, local_heads // GROUP_HEADS)
    all_rows = rows * head_len
    blocks = all_rows // BLOCK
    f32, bf16 = jnp.float32, jnp.bfloat16
    dma = pltpu.SemaphoreType.DMA
    anywhere = pl.BlockSpec(memory_space=pl.ANY)
    in_vmem = pl.BlockSpec(memory_space=pltpu.VMEM)
    return pl.pallas_call(
        functools.partial(kernel, head_len, chain_len),
        out_shape=jax.ShapeDtypeStruct(signal.shape, bf16),
        in_specs=[anywhere] * 4 + [in_vmem] * 2,
        out_specs=anywhere,
        scratch_shapes=[
            pltpu.VMEM((all_rows, cols), bf16),
            pltpu.VMEM((all_rows, groups * SSTATE), bf16),
            pltpu.VMEM((all_rows, groups * SSTATE), bf16),
            pltpu.VMEM((all_rows, HEADS), bf16),
            pltpu.VMEM((blocks, HEADS, BLOCK), f32),
            pltpu.VMEM((blocks * groups, BLOCK, BLOCK), f32),
            pltpu.VMEM((blocks * groups, SSTATE, BLOCK), bf16),
            pltpu.VMEM((HEADS, 128), f32),
            pltpu.VMEM((blocks + 1, SSTATE, cols), f32),
            pltpu.VMEM((blocks + 1, 8, cols), f32),
            pltpu.VMEM((all_rows, cols), f32),
            pltpu.VMEM((all_rows, cols), f32),
            pltpu.VMEM((all_rows, cols), bf16),
            pltpu.VMEM((SSTATE, cols), bf16),
            pltpu.VMEM((SSTATE, cols), bf16),
            dma((3,)), dma((3, head_len)), dma((3, head_len)),
            dma, dma((parts, head_len)), dma((parts, head_len)),
            dma((parts,)), dma((parts,)),
            dma((parts,)), dma((parts, head_len)), dma((parts, head_len)),
        ],
        compiler_params=pltpu.CompilerParams(
            collective_id=0, has_side_effects=True, vmem_limit_bytes=60 * 1024 * 1024
        ),
    )(signal, input_map, output_map, step_size, decay_rate[None, :], skip_gain[None, :])


def solution(mesh):
    return jax.shard_map(
        shards,
        mesh=mesh,
        in_specs=(
            P(("chain", "head"), None),
            P(("chain", "head"), None),
            P(("chain", "head"), None),
            P(("chain", "head"), None),
            P(),
            P(),
        ),
        out_specs=P(("chain", "head"), None),
        check_vma=False,
    )
```

time: 968 us -> 120 us (0.12)
  waiting for transfers between devices: 633 us -> 0 us
  Pallas kernels: 0 us -> 115 us
  local copies, waits for them, and re-layouts: 98.7 us -> 4.57 us
  other arithmetic: 90.5 us -> 0 us
  starting transfers between devices: 63.9 us -> 0 us
  blocking collectives: 58.1 us -> 0 us
  matrix products: 18.4 us -> 0 us
    ppermute x7 -> x0, waiting for transfers between devices: 591 us -> none  [from_behind(): return lax.ppermute(array, axis, pairs)]
    pallas_call x0 -> x1, Pallas kernels: none -> 115 us  [shards(): pl.pallas_call(functools.partial(kernel, head_len, chain_len), out_shape=...]
    all_to_all x1 -> x0, blocking collectives: 58.1 us -> none  [finish(): lax.all_to_all(result, 'head', split_axis=0, concat_axis=1, tiled=True)]
    add x9 -> x0, other arithmetic: 48.5 us -> none  [the longest x7 41.1 us: relay_turn(): leaving = jnp.exp(totals)[:, None, None] * arriving + final_state]
    ppermute x7 -> x0, starting transfers between devices: 46.2 us -> none  [from_behind(): return lax.ppermute(array, axis, pairs)]
    all_to_all x4 -> x0, waiting for transfers between devices: 41.3 us -> none  [the longest x1 28.2 us: shards(): lax.all_to_all(signal, 'head', split_axis=1, concat_axis=0, tiled=True)]
    convert_element_type x5 -> x0, local copies, waits for them, and re-layouts: 39.3 us -> none  [the longest x2 30.5 us: finish(): values_wide = values.astype(jnp.float32)]
    all_to_all x6 -> x0, local copies, waits for them, and re-layouts: 29.2 us -> none  [the longest x3 19.9 us: finish(): lax.all_to_all(result, 'head', split_axis=0, concat_axis=1, tiled=True)]
  transfers between devices with their start and end apart: 11 -> 0, of which waited for: 10 -> 0; matrix products, arithmetic and copies ran while one was open for 3% -> 0% of each run, Pallas kernels for 0% -> 0%
where the time goes in v1:
time: 120 us
  Pallas kernels  115 us (96%)
  local copies, waits for them, and re-layouts  4.57 us (4%)
    pallas_call x1, Pallas kernels, shards(): pl.pallas_call(functools.partial(kernel, head_len, chain_len), out_shape=...  115 us
    unnamed x1, local copies, waits for them, and re-layouts  4.57 us

profile of v1, /device:TPU:1, one launch (start us, length us, event | category | flops | bytes accessed | tf_op | source)
XLA Modules:
  0.0 119.8 jit_solution(7389579711538124745)
XLA Ops:
  0.0 115.2 %shard_map.64 = bf16[128,16384]{1,0:T(8,128)(2,1)} custom-call(bf16[128,16384]{1,0:T(8,128)(2,1)} %signal.1, bf16[128,2048]{1,0:T(8,128)(2,1)} %in_map.1, bf16[128,2048]{1,0:T(8,128)(2,1)} %out_map.1, bf16[128,256]{1,0:T(8,128)(2,1)} %step.1, f32[1,256]{1,0:T(1,128)} %bitcast.2, f32[1,256]{1,0:T(1,128)} %bitcast.3), custom_call_target="tpu_custom_call" | custom-call | tf_op jit(solution)/shard_map/pallas_call | solution.py:307
  115.2 4.6 %copy.8 = bf16[128,16384]{1,0:T(8,128)(2,1)} copy(bf16[128,16384]{1,0:T(8,128)(2,1)} %shard_map.64) | data formatting | bytes 8388608
